TPU v7x, 512 devices: a whole 4x4x16 slice. The times are simulated.
512 devices in a mesh: ctx: 64 (over z_lo, y, x), tp: 8 (over z_hi, core).
Axes of the slice: x: 4, y: 4, z: 16 (z_hi: 4, z_lo: 4; z = z_hi * 4 + z_lo), core: 2. Of those that a mesh axis runs over, the one named last changes fastest.
Arguments:
- query: bfloat16 [32768, 4096], P(('ctx', 'tp')), may hold values from -6 to 6
- key_states: bfloat16 [32768, 1024], P(('ctx', 'tp')), may hold values from -6 to 6
- value_states: bfloat16 [32768, 1024], P(('ctx', 'tp')), may hold values from -6 to 6
- grad_out: bfloat16 [32768, 4096], P(('ctx', 'tp')), may hold values from -6 to 6
- segment_ids: int32 [32768], replicated, may hold values from 0 to 34, as said below
Outputs:
- attention_out: bfloat16 [32768, 4096], P('ctx', 'tp')
- query_grad: bfloat16 [32768, 4096], P('ctx', 'tp')
- key_grad: bfloat16 [32768, 1024], P('ctx', 'tp')
- value_grad: bfloat16 [32768, 1024], P('ctx', 'tp')
Inputs may be any that keep to these rules, and one draw needn't show every extreme that they name: `segment_ids`: never falling along the tokens, starting at 0 and rising by one at each new document; every document has 1 to 1024 tokens, and one has exactly 1024.
All inputs are finite; a program needn't handle non-finite values.
Results may differ from a plain program's by a relative error of at most 0.035.
Values may be sent and summed in bfloat16 or wider, within the bound.
A program may use at most 64 MiB of HBM per device.

v0:
```python
import jax
import jax.numpy as jnp
from jax import lax
from jax.sharding import PartitionSpec as P

QH = 32
KVH = 8
HD = 128


NEGATIVE = -1e30


def shifted(value, axis, steps):
    count = lax.axis_size(axis)
    leading, last = (max(0, -steps), min(count, count - steps))
    return lax.ppermute(value, axis, [(source, source + steps) for source in range(leading, last)])


def block_scores(head_query, keys, allowed, scaling):
    scores = jnp.einsum("qd,kd->qk", head_query, keys, preferred_element_type=jnp.float32) * scaling
    return jnp.where(allowed, scores, NEGATIVE)


def weighted_sum(weights, values):
    return jnp.dot(weights, values, preferred_element_type=jnp.float32)


def backward_block(head_query, head_grad, keys, values, probs_part, half_part, row_delta, scaling):
    grad_probs = jnp.einsum("qd,kd->qk", head_grad, values, preferred_element_type=jnp.float32)
    slopes = (probs_part * (grad_probs - row_delta[:, None])).astype(jnp.bfloat16)
    query_term = jnp.dot(slopes, keys, preferred_element_type=jnp.float32)
    key_term = (
        jnp.einsum("qk,qd->kd", slopes, head_query, preferred_element_type=jnp.float32) * scaling
    )
    value_term = jnp.einsum("qk,qd->kd", half_part, head_grad, preferred_element_type=jnp.float32)
    return (query_term, key_term, value_term)


def on_device(query, key_states, value_states, grad_out, segment_ids):
    tp_count = lax.axis_size("tp")
    heads_here = QH // tp_count
    kv_here = KVH // tp_count
    group_size = QH // KVH
    scaling = HD ** (-0.5)
    query_local, key_local, value_local, grads_local = (
        lax.all_to_all(query, "tp", split_axis=1, concat_axis=0, tiled=True),
        lax.all_to_all(key_states, "tp", split_axis=1, concat_axis=0, tiled=True),
        lax.all_to_all(value_states, "tp", split_axis=1, concat_axis=0, tiled=True),
        lax.all_to_all(grad_out, "tp", split_axis=1, concat_axis=0, tiled=True),
    )
    tokens_here = query_local.shape[0]
    position = lax.axis_index("ctx")
    segs_padded = jnp.concatenate([jnp.full((2 * tokens_here,), -1, jnp.int32), segment_ids])
    key_segs = lax.dynamic_slice_in_dim(segs_padded, position * tokens_here, 3 * tokens_here, 0)
    query_segs = key_segs[2 * tokens_here :]
    near_keys, near_values = shifted((key_local, value_local), "ctx", 1)
    far_keys, far_values = shifted((key_local, value_local), "ctx", 2)
    key_window = (
        jnp.concatenate([far_keys, near_keys, key_local], 0)
        .reshape(3 * tokens_here, kv_here, HD)
        .transpose(1, 0, 2)
    )
    value_window = (
        jnp.concatenate([far_values, near_values, value_local], 0)
        .reshape(3 * tokens_here, kv_here, HD)
        .transpose(1, 0, 2)
    )
    row_ids = jnp.arange(tokens_here, dtype=jnp.int32) + 2 * tokens_here
    masks = []
    for block in range(3):
        col_ids = jnp.arange(tokens_here, dtype=jnp.int32) + block * tokens_here
        block_segs = key_segs[block * tokens_here : (block + 1) * tokens_here]
        masks.append(
            (query_segs[:, None] == block_segs[None, :]) & (col_ids[None, :] <= row_ids[:, None])
        )
    head_queries = query_local.reshape(tokens_here, heads_here, HD).transpose(1, 0, 2)
    head_grads = grads_local.reshape(tokens_here, heads_here, HD).transpose(1, 0, 2)

    def head_step(carry, inputs):
        key_accum, value_accum = carry
        head_query, head_grad, head_index = inputs
        kv_index = head_index // group_size
        head_keys = lax.dynamic_index_in_dim(key_window, kv_index, 0, keepdims=False)
        head_values = lax.dynamic_index_in_dim(value_window, kv_index, 0, keepdims=False)
        key_blocks = []
        value_blocks = []
        score_list = []
        for block in range(3):
            key_blocks.append(head_keys[block * tokens_here : (block + 1) * tokens_here])
            value_blocks.append(head_values[block * tokens_here : (block + 1) * tokens_here])
            score_list.append(block_scores(head_query, key_blocks[block], masks[block], scaling))
        scores = jnp.concatenate(score_list, 1)
        peak = jnp.max(scores, axis=-1, keepdims=True)
        expos = jnp.exp(scores - peak)
        probs = expos / jnp.sum(expos, axis=-1, keepdims=True)
        probs_half = probs.astype(jnp.bfloat16)
        out_sum = jnp.zeros((tokens_here, HD), jnp.float32)
        for block in range(3):
            weights = probs_half[:, block * tokens_here : (block + 1) * tokens_here]
            out_sum = out_sum + weighted_sum(weights, value_blocks[block])
        attended = out_sum.astype(jnp.bfloat16)
        row_delta = jnp.sum(head_grad.astype(jnp.float32) * attended.astype(jnp.float32), axis=-1)
        query_sum = jnp.zeros((tokens_here, HD), jnp.float32)
        key_parts = []
        value_parts = []
        for block in range(3):
            lower = block * tokens_here
            upper = lower + tokens_here
            terms = backward_block(
                head_query,
                head_grad,
                key_blocks[block],
                value_blocks[block],
                probs[:, lower:upper],
                probs_half[:, lower:upper],
                row_delta,
                scaling,
            )
            query_sum = query_sum + terms[0]
            key_parts.append(terms[1])
            value_parts.append(terms[2])
        query_grad_head = (query_sum * scaling).astype(jnp.bfloat16)
        key_current = lax.dynamic_index_in_dim(key_accum, kv_index, 0, keepdims=False)
        value_current = lax.dynamic_index_in_dim(value_accum, kv_index, 0, keepdims=False)
        key_accum = lax.dynamic_update_index_in_dim(
            key_accum, key_current + jnp.concatenate(key_parts, 0), kv_index, 0
        )
        value_accum = lax.dynamic_update_index_in_dim(
            value_accum, value_current + jnp.concatenate(value_parts, 0), kv_index, 0
        )
        return ((key_accum, value_accum), (attended, query_grad_head))

    initial = jnp.zeros((kv_here, 3 * tokens_here, HD), jnp.float32)
    (key_accum, value_accum), (attended_all, query_all) = lax.scan(
        head_step,
        (initial, initial),
        (head_queries, head_grads, jnp.arange(heads_here, dtype=jnp.int32)),
    )
    attention_out = attended_all.transpose(1, 0, 2).reshape(tokens_here, heads_here * HD)
    query_grad = query_all.transpose(1, 0, 2).reshape(tokens_here, heads_here * HD)
    key_terms = key_accum.transpose(1, 0, 2).reshape(3 * tokens_here, kv_here * HD)
    value_terms = value_accum.transpose(1, 0, 2).reshape(3 * tokens_here, kv_here * HD)
    key_far = key_terms[:tokens_here]
    key_near = key_terms[tokens_here : 2 * tokens_here]
    key_own = key_terms[2 * tokens_here :]
    value_far = value_terms[:tokens_here]
    value_near = value_terms[tokens_here : 2 * tokens_here]
    value_own = value_terms[2 * tokens_here :]
    near_keys_back, near_values_back = (
        shifted(key_near.astype(jnp.bfloat16), "ctx", -1).astype(key_near.dtype),
        shifted(value_near.astype(jnp.bfloat16), "ctx", -1).astype(value_near.dtype),
    )
    far_keys_back, far_values_back = (
        shifted(key_far.astype(jnp.bfloat16), "ctx", -2).astype(key_far.dtype),
        shifted(value_far.astype(jnp.bfloat16), "ctx", -2).astype(value_far.dtype),
    )
    key_total = key_own + near_keys_back + far_keys_back
    value_total = value_own + near_values_back + far_values_back
    return (
        attention_out,
        query_grad,
        key_total.astype(jnp.bfloat16),
        value_total.astype(jnp.bfloat16),
    )


def solution(mesh):
    in_specs = (
        P(("ctx", "tp"), None),
        P(("ctx", "tp"), None),
        P(("ctx", "tp"), None),
        P(("ctx", "tp"), None),
        P(),
    )
    out_specs = (P("ctx", "tp"), P("ctx", "tp"), P("ctx", "tp"), P("ctx", "tp"))
    return jax.shard_map(
        on_device, mesh=mesh, in_specs=in_specs, out_specs=out_specs, check_vma=False
    )
```

profile of v0, /device:TPU:40, one launch (start us, length us, event | category | flops | bytes accessed | tf_op | source)
XLA Modules:
  0.0 254.7 jit_solution(11648641449808474122)
XLA Ops:
  2.2 14.2 %all-to-all-start.1 = ((bf16[64,8,128]{2,0,1:T(8,128)(2,1)}), bf16[64,8,128]{2,0,1:T(8,128)(2,1)S(1)}, u32[]{:S(2)}, u32[]{:S(2)}) async-start(bf16[64,8,128]{2,0,1:T(8,128)(2,1)} %copy_bitcast_fusion.4), calls=%async_computation.1 | async-start | bytes 262144 | tf_op jit(solution)/shard_map/all_to_all | solution.py:48
  16.4 1.6 copy_bitcast_fusion.3
  18.0 15.6 %all-to-all-done.1 = bf16[64,8,128]{2,0,1:T(8,128)(2,1)S(1)} async-done(((bf16[64,8,128]{2,0,1:T(8,128)(2,1)}), bf16[64,8,128]{2,0,1:T(8,128)(2,1)S(1)}, u32[]{:S(2)}, u32[]{:S(2)}) %all-to-all-start.1) | async-done | bytes 131104 | tf_op jit(solution)/shard_map/all_to_all | solution.py:48
  33.6 3.4 %all-to-all-start.3 = ((bf16[64,8,128]{2,0,1:T(8,128)(2,1)}), bf16[64,8,128]{2,0,1:T(8,128)(2,1)S(1)}, u32[]{:S(2)}, u32[]{:S(2)}) async-start(bf16[64,8,128]{2,0,1:T(8,128)(2,1)} %copy_bitcast_fusion.3), calls=%async_computation.3 | async-start | bytes 262144 | tf_op jit(solution)/shard_map/all_to_all | solution.py:49
  37.0 1.9 copy.45
  38.9 14.7 %all-to-all-done.3 = bf16[64,8,128]{2,0,1:T(8,128)(2,1)S(1)} async-done(((bf16[64,8,128]{2,0,1:T(8,128)(2,1)}), bf16[64,8,128]{2,0,1:T(8,128)(2,1)S(1)}, u32[]{:S(2)}, u32[]{:S(2)}) %all-to-all-start.3) | async-done | bytes 131104 | tf_op jit(solution)/shard_map/all_to_all | solution.py:49
  53.6 3.5 %all-to-all-start = ((bf16[64,8,512]{2,0,1:T(8,128)(2,1)}), bf16[64,8,512]{2,0,1:T(8,128)(2,1)S(1)}, u32[]{:S(2)}, u32[]{:S(2)}) async-start(bf16[64,8,512]{2,0,1:T(8,128)(2,1)} %bitcast.155), calls=%async_computation | async-start | bytes 1048576 | tf_op jit(solution)/shard_map/all_to_all | solution.py:47
  58.0 31.0 %all-to-all-done = bf16[64,8,512]{2,0,1:T(8,128)(2,1)S(1)} async-done(((bf16[64,8,512]{2,0,1:T(8,128)(2,1)}), bf16[64,8,512]{2,0,1:T(8,128)(2,1)S(1)}, u32[]{:S(2)}, u32[]{:S(2)}) %all-to-all-start) | async-done | bytes 524320 | tf_op jit(solution)/shard_map/all_to_all | solution.py:47
  89.0 3.5 %all-to-all-start.2 = ((bf16[64,8,512]{2,0,1:T(8,128)(2,1)}), bf16[64,8,512]{2,0,1:T(8,128)(2,1)S(1)}, u32[]{:S(2)}, u32[]{:S(2)}) async-start(bf16[64,8,512]{2,0,1:T(8,128)(2,1)} %bitcast.154), calls=%async_computation.2 | async-start | bytes 1048576 | tf_op jit(solution)/shard_map/all_to_all | solution.py:50
  92.5 5.0 %collective-permute-start = (bf16[512,128]{1,0:T(8,128)(2,1)S(1)}, bf16[512,128]{1,0:T(8,128)(2,1)S(1)}, u32[]{:S(2)}, u32[]{:S(2)}) collective-permute-start(bf16[512,128]{1,0:T(8,128)(2,1)S(1)} %bitcast.240), channel_id=1, source_target_pairs={{0,16},{8,24},{16,32},{24,40},{32,48},{40,56},{48,64},{56,72},{64,... | collective-permute-start | bytes 393224 | tf_op jit(solution)/shard_map/ppermute | solution.py:17
  97.5 2.5 collective-permute-start.1
  100.7 4.9 %collective-permute-start.2 = (bf16[512,128]{1,0:T(8,128)(2,1)S(1)}, bf16[512,128]{1,0:T(8,128)(2,1)S(1)}, u32[]{:S(2)}, u32[]{:S(2)}) collective-permute-start(bf16[512,128]{1,0:T(8,128)(2,1)S(1)} %bitcast.243), channel_id=1, source_target_pairs={{0,16},{8,24},{16,32},{24,40},{32,48},{40,56},{48,64},{56,72},{64,... | collective-permute-start | bytes 393224 | tf_op jit(solution)/shard_map/ppermute | solution.py:17
  105.6 3.4 %collective-permute-start.3 = (bf16[512,128]{1,0:T(8,128)(2,1)S(1)}, bf16[512,128]{1,0:T(8,128)(2,1)S(1)}, u32[]{:S(2)}, u32[]{:S(2)}) collective-permute-start(bf16[512,128]{1,0:T(8,128)(2,1)S(1)} %bitcast.244), channel_id=1, source_target_pairs={{0,8},{8,16},{16,24},{24,32},{32,40},{40,48},{48,56},{56,64},{64,7... | collective-permute-start | bytes 393224 | tf_op jit(solution)/shard_map/ppermute | solution.py:17
  110.2 4.4 %collective-permute-done.3 = bf16[512,128]{1,0:T(8,128)(2,1)S(1)} collective-permute-done((bf16[512,128]{1,0:T(8,128)(2,1)S(1)}, bf16[512,128]{1,0:T(8,128)(2,1)S(1)}, u32[]{:S(2)}, u32[]{:S(2)}) %collective-permute-start.3) | collective-permute-done | bytes 131104 | tf_op jit(solution)/shard_map/ppermute | solution.py:17
  116.3 8.7 %all-to-all-done.2 = bf16[64,8,512]{2,0,1:T(8,128)(2,1)S(1)} async-done(((bf16[64,8,512]{2,0,1:T(8,128)(2,1)}), bf16[64,8,512]{2,0,1:T(8,128)(2,1)S(1)}, u32[]{:S(2)}, u32[]{:S(2)}) %all-to-all-start.2) | async-done | bytes 524320 | tf_op jit(solution)/shard_map/all_to_all | solution.py:50
  125.5 99.0 %while.20 = (s32[]{:T(128)}, f32[1,1536,128]{2,1,0:T(8,128)S(1)}, f32[1,1536,128]{2,1,0:T(8,128)S(1)}, bf16[4,512,128]{1,2,0:T(8,128)(2,1)}, bf16[4,512,128]{2,1...) while((s32[]{:T(128)}, f32[1,1536,128]{2,1,0:T(8,128)S(1)}, ...), condition=%wide.region_6.7_spmd.clone.clone.clone, body=%wide.region_0.6_spmd.clone.clone.clone.sunk | while | flops 1224604160 | bytes 37939396 | solution.py:135
  133.0 1.9 multiply_reduce_fusion.2
  141.0 1.9 fusion.196
  148.1 1.5 maximum_add_fusion.3
  157.8 1.9 multiply_reduce_fusion.2
  165.7 1.9 fusion.196
  172.8 1.5 maximum_add_fusion.3
  182.5 1.9 multiply_reduce_fusion.2
  190.4 1.9 fusion.196
  207.3 1.9 multiply_reduce_fusion.2
  215.2 1.9 fusion.196
  224.6 4.7 %collective-permute-start.6 = (bf16[512,128]{1,0:T(8,128)(2,1)S(1)}, bf16[512,128]{1,0:T(8,128)(2,1)S(1)}, u32[]{:S(2)}, u32[]{:S(2)}) collective-permute-start(bf16[512,128]{1,0:T(8,128)(2,1)S(1)} %get-tuple-element.310), channel_id=1, source_target_pairs={{8,0},{16,8},{24,16},{32,24},{40,32},{48,40},{56,48},{64,56},{72,6... | collective-permute-start | bytes 393224 | tf_op jit(solution)/shard_map/ppermute | solution.py:17
  229.3 10.0 %collective-permute-start.7 = (bf16[512,128]{1,0:T(8,128)(2,1)S(1)}, bf16[512,128]{1,0:T(8,128)(2,1)S(1)}, u32[]{:S(2)}, u32[]{:S(2)}) collective-permute-start(bf16[512,128]{1,0:T(8,128)(2,1)S(1)} %get-tuple-element.311), channel_id=1, source_target_pairs={{16,0},{24,8},{32,16},{40,24},{48,32},{56,40},{64,48},{72,56},{80,... | collective-permute-start | bytes 393224 | tf_op jit(solution)/shard_map/ppermute | solution.py:17
  239.4 6.3 %collective-permute-start.4 = (bf16[512,128]{1,0:T(8,128)(2,1)S(1)}, bf16[512,128]{1,0:T(8,128)(2,1)S(1)}, u32[]{:S(2)}, u32[]{:S(2)}) collective-permute-start(bf16[512,128]{1,0:T(8,128)(2,1)S(1)} %get-tuple-element.312), channel_id=1, source_target_pairs={{8,0},{16,8},{24,16},{32,24},{40,32},{48,40},{56,48},{64,56},{72,6... | collective-permute-start | bytes 393224 | tf_op jit(solution)/shard_map/ppermute | solution.py:17
  245.6 1.9 collective-permute-start.5
  247.6 2.0 copy.33
  251.2 2.8 %collective-permute-done.5 = bf16[512,128]{1,0:T(8,128)(2,1)S(1)} collective-permute-done((bf16[512,128]{1,0:T(8,128)(2,1)S(1)}, bf16[512,128]{1,0:T(8,128)(2,1)S(1)}, u32[]{:S(2)}, u32[]{:S(2)}) %collective-permute-start.5) | collective-permute-done | bytes 131104 | tf_op jit(solution)/shard_map/ppermute | solution.py:17
  (125 shorter events, 89.3 us)
Async XLA Ops:
  0.6 0.9 copy-start
  0.6 56.5 %copy-start.2 = (bf16[64,4096]{1,0:T(8,128)(2,1)S(1)}, bf16[64,4096]{1,0:T(8,128)(2,1)}, u32[]{:S(2)}) copy-start(bf16[64,4096]{1,0:T(8,128)(2,1)} %param.10) | copy-start | bytes 1572868
  1.5 99.0 %copy-start.4 = (s32[32768]{0:T(1024)S(1)}, s32[32768]{0:T(1024)}, u32[]{:S(2)}) copy-start(s32[32768]{0:T(1024)} %param.11) | copy-start | bytes 393220
  2.2 31.4 %all-to-all-start.1 = ((bf16[64,8,128]{2,0,1:T(8,128)(2,1)}), bf16[64,8,128]{2,0,1:T(8,128)(2,1)S(1)}, u32[]{:S(2)}, u32[]{:S(2)}) async-start(bf16[64,8,128]{2,0,1:T(8,128)(2,1)} %copy_bitcast_fusion.4), calls=%async_computation.1 | async-start | bytes 262144 | tf_op jit(solution)/shard_map/all_to_all | solution.py:48
  33.6 20.0 %all-to-all-start.3 = ((bf16[64,8,128]{2,0,1:T(8,128)(2,1)}), bf16[64,8,128]{2,0,1:T(8,128)(2,1)S(1)}, u32[]{:S(2)}, u32[]{:S(2)}) async-start(bf16[64,8,128]{2,0,1:T(8,128)(2,1)} %copy_bitcast_fusion.3), calls=%async_computation.3 | async-start | bytes 262144 | tf_op jit(solution)/shard_map/all_to_all | solution.py:49
  53.6 35.4 %all-to-all-start = ((bf16[64,8,512]{2,0,1:T(8,128)(2,1)}), bf16[64,8,512]{2,0,1:T(8,128)(2,1)S(1)}, u32[]{:S(2)}, u32[]{:S(2)}) async-start(bf16[64,8,512]{2,0,1:T(8,128)(2,1)} %bitcast.155), calls=%async_computation | async-start | bytes 1048576 | tf_op jit(solution)/shard_map/all_to_all | solution.py:47
  89.0 36.0 %all-to-all-start.2 = ((bf16[64,8,512]{2,0,1:T(8,128)(2,1)}), bf16[64,8,512]{2,0,1:T(8,128)(2,1)S(1)}, u32[]{:S(2)}, u32[]{:S(2)}) async-start(bf16[64,8,512]{2,0,1:T(8,128)(2,1)} %bitcast.154), calls=%async_computation.2 | async-start | bytes 1048576 | tf_op jit(solution)/shard_map/all_to_all | solution.py:50
  92.5 16.5 %collective-permute-start = (bf16[512,128]{1,0:T(8,128)(2,1)S(1)}, bf16[512,128]{1,0:T(8,128)(2,1)S(1)}, u32[]{:S(2)}, u32[]{:S(2)}) collective-permute-start(bf16[512,128]{1,0:T(8,128)(2,1)S(1)} %bitcast.240), channel_id=1, source_target_pairs={{0,16},{8,24},{16,32},{24,40},{32,48},{40,56},{48,64},{56,72},{64,... | collective-permute-start | bytes 393224 | tf_op jit(solution)/shard_map/ppermute | solution.py:17
  97.5 11.5 %collective-permute-start.1 = (bf16[512,128]{1,0:T(8,128)(2,1)S(1)}, bf16[512,128]{1,0:T(8,128)(2,1)S(1)}, u32[]{:S(2)}, u32[]{:S(2)}) collective-permute-start(bf16[512,128]{1,0:T(8,128)(2,1)S(1)} %bitcast.241), channel_id=1, source_target_pairs={{0,8},{8,16},{16,24},{24,32},{32,40},{40,48},{48,56},{56,64},{64,7... | collective-permute-start | bytes 393224 | tf_op jit(solution)/shard_map/ppermute | solution.py:17
  100.7 9.5 %collective-permute-start.2 = (bf16[512,128]{1,0:T(8,128)(2,1)S(1)}, bf16[512,128]{1,0:T(8,128)(2,1)S(1)}, u32[]{:S(2)}, u32[]{:S(2)}) collective-permute-start(bf16[512,128]{1,0:T(8,128)(2,1)S(1)} %bitcast.243), channel_id=1, source_target_pairs={{0,16},{8,24},{16,32},{24,40},{32,48},{40,56},{48,64},{56,72},{64,... | collective-permute-start | bytes 393224 | tf_op jit(solution)/shard_map/ppermute | solution.py:17
  105.6 9.0 %collective-permute-start.3 = (bf16[512,128]{1,0:T(8,128)(2,1)S(1)}, bf16[512,128]{1,0:T(8,128)(2,1)S(1)}, u32[]{:S(2)}, u32[]{:S(2)}) collective-permute-start(bf16[512,128]{1,0:T(8,128)(2,1)S(1)} %bitcast.244), channel_id=1, source_target_pairs={{0,8},{8,16},{16,24},{24,32},{32,40},{40,48},{48,56},{56,64},{64,7... | collective-permute-start | bytes 393224 | tf_op jit(solution)/shard_map/ppermute | solution.py:17
  148.1 1.5 copy-start.1
  172.8 1.5 copy-start.1
  197.6 1.5 copy-start.1
  222.3 1.5 copy-start.1
  224.5 25.1 %copy-start.3 = (bf16[4,512,128]{2,1,0:T(8,128)(2,1)S(1)}, bf16[4,512,128]{2,1,0:T(8,128)(2,1)}, u32[]{:S(2)}) copy-start(bf16[4,512,128]{2,1,0:T(8,128)(2,1)} %get-tuple-element.98) | copy-start | bytes 1572868
  224.6 25.9 %collective-permute-start.6 = (bf16[512,128]{1,0:T(8,128)(2,1)S(1)}, bf16[512,128]{1,0:T(8,128)(2,1)S(1)}, u32[]{:S(2)}, u32[]{:S(2)}) collective-permute-start(bf16[512,128]{1,0:T(8,128)(2,1)S(1)} %get-tuple-element.310), channel_id=1, source_target_pairs={{8,0},{16,8},{24,16},{32,24},{40,32},{48,40},{56,48},{64,56},{72,6... | collective-permute-start | bytes 393224 | tf_op jit(solution)/shard_map/ppermute | solution.py:17
  229.3 21.2 %collective-permute-start.7 = (bf16[512,128]{1,0:T(8,128)(2,1)S(1)}, bf16[512,128]{1,0:T(8,128)(2,1)S(1)}, u32[]{:S(2)}, u32[]{:S(2)}) collective-permute-start(bf16[512,128]{1,0:T(8,128)(2,1)S(1)} %get-tuple-element.311), channel_id=1, source_target_pairs={{16,0},{24,8},{32,16},{40,24},{48,32},{56,40},{64,48},{72,56},{80,... | collective-permute-start | bytes 393224 | tf_op jit(solution)/shard_map/ppermute | solution.py:17
  239.4 11.8 %collective-permute-start.4 = (bf16[512,128]{1,0:T(8,128)(2,1)S(1)}, bf16[512,128]{1,0:T(8,128)(2,1)S(1)}, u32[]{:S(2)}, u32[]{:S(2)}) collective-permute-start(bf16[512,128]{1,0:T(8,128)(2,1)S(1)} %get-tuple-element.312), channel_id=1, source_target_pairs={{8,0},{16,8},{24,16},{32,24},{40,32},{48,40},{56,48},{64,56},{72,6... | collective-permute-start | bytes 393224 | tf_op jit(solution)/shard_map/ppermute | solution.py:17
  245.6 8.4 %collective-permute-start.5 = (bf16[512,128]{1,0:T(8,128)(2,1)S(1)}, bf16[512,128]{1,0:T(8,128)(2,1)S(1)}, u32[]{:S(2)}, u32[]{:S(2)}) collective-permute-start(bf16[512,128]{1,0:T(8,128)(2,1)S(1)} %get-tuple-element.313), channel_id=1, source_target_pairs={{16,0},{24,8},{32,16},{40,24},{48,32},{56,40},{64,48},{72,56},{80,... | collective-permute-start | bytes 393224 | tf_op jit(solution)/shard_map/ppermute | solution.py:17
where the time goes:
time: 257 us; the launch traced here: 255 us
  matrix products  85.8 us (33%)
  waiting for transfers between devices  77.7 us (30%)
  starting transfers between devices  63.2 us (25%)
  other arithmetic  13.8 us (5%)
  local copies, waits for them, and re-layouts  13 us (5%)
    ppermute x8, starting transfers between devices, shifted(): lax.ppermute(value, axis, [(source, source + steps) for source in range(l...  38.7 us
    all_to_all x1, waiting for transfers between devices, on_device(): lax.all_to_all(query, 'tp', split_axis=1, concat_axis=0, tiled=True)  31 us
    dot_general x12, matrix products, backward_block(): query_term = jnp.dot(slopes, keys, preferred_element_type=jnp.float32)  17.6 us
    dot_general x12, matrix products, weighted_sum(): return jnp.dot(weights, values, preferred_element_type=jnp.float32)  16.8 us
    dot_general x12, matrix products, block_scores(): jnp.einsum('qd,kd->qk', head_query, keys, preferred_element_type=jnp.floa...  16.3 us
    all_to_all x1, waiting for transfers between devices, on_device(): lax.all_to_all(key_states, 'tp', split_axis=1, concat_axis=0, tiled=True)  15.6 us
    all_to_all x1, waiting for transfers between devices, on_device(): lax.all_to_all(value_states, 'tp', split_axis=1, concat_axis=0, tiled=True)  14.7 us
    dot_general x12, matrix products, backward_block(): jnp.einsum('qk,qd->kd', slopes, head_query, preferred_element_type=jnp.fl...  14.4 us
  transfers between devices with their start and end apart: 12, of which 7 were waited for; matrix products, arithmetic and copies ran while one was open for 4% of the time, Pallas kernels for 0%

commit v1 on v0

v1 whole, which is shorter than its diff:
```python
import math

import jax
import jax.numpy as jnp
from jax import lax
from jax.experimental import pallas as pl
from jax.experimental.pallas import tpu as pltpu
from jax.sharding import PartitionSpec as P

QH = 32
KVH = 8
HD = 128
TOK = 512
SUB = 64
GROUP = QH // KVH
CTX = 64
TP = 8
LANES = SUB * GROUP
WIN = 1152
TILE = 128
TILES = WIN // TILE
NEGATIVE = -1e30
MESH = pl.DeviceIdType.MESH
SCALING = HD**-0.5
EXP_SCALE = SCALING * math.log2(math.e)

NT = (((1,), (1,)), ((), ()))


def dot(a, b):
    return jnp.dot(a, b, preferred_element_type=jnp.float32)


def dot_nt(a, b):
    return lax.dot_general(a, b, NT, preferred_element_type=jnp.float32)


def fold(x, op):
    parts = [x[i * 8 : (i + 1) * 8] for i in range(x.shape[0] // 8)]
    while len(parts) > 1:
        parts = [op(parts[i], parts[i + 1]) for i in range(0, len(parts), 2)]
    return parts[0]


def kernel(
    q_in,
    k_in,
    v_in,
    g_in,
    seg_in,
    out_ref,
    dq_ref,
    dk_ref,
    dv_ref,
    qbuf,
    gbuf,
    kv,
    kvt,
    segcol,
    segrow,
    s_scr,
    p_scr,
    e_scr,
    acc,
    tx,
    rx,
    q_send,
    q_recv,
    g_send,
    g_recv,
    k_send,
    k_recv,
    v_send,
    v_recv,
    w_send,
    w_recv,
    t_send,
    t_recv,
):
    c = lax.axis_index("ctx")
    t = lax.axis_index("tp")
    zh, co = t // 2, t % 2

    barrier = pltpu.get_barrier_semaphore()
    for d in range(1, TP):
        pl.semaphore_signal(barrier, inc=1, device_id={"tp": (t + d) % TP}, device_id_type=MESH)
    for d in (1, 2, CTX - 1, CTX - 2):
        pl.semaphore_signal(barrier, inc=1, device_id={"ctx": (c + d) % CTX}, device_id_type=MESH)

    def narrow(ref, j):
        return ref.at[:, pl.ds(pl.multiple_of(j * HD, HD), HD)]

    def wide(ref, j):
        return ref.at[:, pl.ds(pl.multiple_of(j * GROUP * HD, GROUP * HD), GROUP * HD)]

    def own_rows(j):
        return pl.ds(pl.multiple_of(2 * TOK + j * SUB, SUB), SUB)

    pltpu.make_async_copy(narrow(k_in, t), kv.at[0, own_rows(t)], k_recv.at[t]).start()
    pltpu.make_async_copy(narrow(v_in, t), kv.at[1, own_rows(t)], v_recv.at[t]).start()
    pltpu.make_async_copy(wide(q_in, t), qbuf.at[t], q_recv.at[t]).start()
    pltpu.make_async_copy(wide(g_in, t), gbuf.at[t], g_recv.at[t]).start()

    @pl.when(c < 1)
    def _():
        kv[:, TOK : 2 * TOK] = jnp.zeros((2, TOK, HD), jnp.bfloat16)

    @pl.when(c < 2)
    def _():
        kv[:, 0:TOK] = jnp.zeros((2, TOK, HD), jnp.bfloat16)

    acc[...] = jnp.zeros_like(acc)

    for block in range(3):
        at = jnp.maximum(c - 2 + block, 0)
        rows = seg_in[pl.ds(pl.multiple_of(at * 4, 4), 4), :].astype(jnp.float32)
        rows = jnp.where(c - 2 + block >= 0, rows, -1.0)
        for i in range(4):
            wide_row = jnp.broadcast_to(rows[i : i + 1], (TILE, TILE))
            start = block * TOK + i * TILE
            segcol[start : start + TILE, :] = wide_row.T
    own = seg_in[pl.ds(pl.multiple_of(c * 4, 4), 4), :].astype(jnp.float32)
    low_lane = lax.broadcasted_iota(jnp.int32, (8, TILE), 1) < SUB
    for i in range(4):
        row = jnp.broadcast_to(own[i : i + 1], (8, TILE))
        turned = pltpu.roll(row, SUB, 1)
        low = jnp.where(low_lane, row, turned)
        high = jnp.where(low_lane, turned, row)
        segrow[2 * i] = jnp.concatenate([low, low], 1)
        segrow[2 * i + 1] = jnp.concatenate([high, high], 1)

    pl.semaphore_wait(barrier, TP - 1 + 4)

    def partner(dz, dc):
        return ((zh + dz) % 4) * 2 + (co + dc) % 2

    partners = [(1, 0), (3, 0), (1, 1), (3, 1), (2, 0), (2, 1), (0, 1)]

    def exchange(src, dst, send, recv, to):
        return pltpu.make_async_remote_copy(
            src_ref=src,
            dst_ref=dst,
            send_sem=send.at[to],
            recv_sem=recv.at[t],
            device_id={"tp": to},
            device_id_type=MESH,
        )

    def key_copies(to):
        return (
            exchange(narrow(k_in, to), kv.at[0, own_rows(t)], k_send, k_recv, to),
            exchange(narrow(v_in, to), kv.at[1, own_rows(t)], v_send, v_recv, to),
        )

    def query_copies(to):
        return (
            exchange(wide(q_in, to), qbuf.at[t], q_send, q_recv, to),
            exchange(wide(g_in, to), gbuf.at[t], g_send, g_recv, to),
        )

    for dz, dc in partners:
        for copy in key_copies(partner(dz, dc)):
            copy.start()
    for dz, dc in partners:
        for copy in query_copies(partner(dz, dc)):
            copy.start()

    def wait_key(j, carry):
        pltpu.make_async_copy(kv.at[0, own_rows(j)], kv.at[0, own_rows(j)], k_recv.at[j]).wait()
        pltpu.make_async_copy(kv.at[1, own_rows(j)], kv.at[1, own_rows(j)], v_recv.at[j]).wait()
        return carry

    lax.fori_loop(0, TP, wait_key, 0)

    def window_copy(d):
        return pltpu.make_async_remote_copy(
            src_ref=kv.at[:, pl.ds(2 * TOK, TOK)],
            dst_ref=kv.at[:, pl.ds((2 - d) * TOK, TOK)],
            send_sem=w_send.at[d - 1],
            recv_sem=w_recv.at[d - 1],
            device_id={"ctx": (c + d) % CTX},
            device_id_type=MESH,
        )

    for d in (1, 2):

        @pl.when(c < CTX - d)
        def _():
            window_copy(d).start()

    def turn(start):
        for i in range(TOK // TILE):
            at = start + i * TILE
            for w in range(2):
                block = kv[w, at : at + TILE, :].astype(jnp.float32)
                kvt[w, :, at : at + TILE] = block.T.astype(jnp.bfloat16)

    turn(2 * TOK)
    for d in (1, 2):

        @pl.when(c >= d)
        def _():
            window_copy(d).wait_recv()

        turn((2 - d) * TOK)

    lane = lax.broadcasted_iota(jnp.int32, (TILE, LANES), 1) % SUB
    place = lax.broadcasted_iota(jnp.int32, (TILE, LANES), 0)

    def unit(i, carry):
        a = i // 2
        dz = a + a // 2 - 2 * (a // 3)
        sz, sc = (zh + dz) % 4, (co + i) % 2
        j = sz * 2 + sc
        pltpu.make_async_copy(qbuf.at[j], qbuf.at[j], q_recv.at[j]).wait()
        pltpu.make_async_copy(gbuf.at[j], gbuf.at[j], g_recv.at[j]).wait()
        base = pl.multiple_of(sz * TILE, TILE)

        def keys(n):
            return pl.ds(pl.multiple_of(base + n * TILE, TILE), TILE)

        qs = jnp.concatenate([qbuf[j, :, h * HD : (h + 1) * HD] for h in range(GROUP)], 0)
        gs = jnp.concatenate([gbuf[j, :, h * HD : (h + 1) * HD] for h in range(GROUP)], 0)
        seg_q = segrow[j][0:1]
        causal = place <= lane + sc * SUB

        peak = None
        for n in range(TILES):
            s = dot_nt(kv[0, keys(n), :], qs)
            seg_k = segcol[keys(n), :]
            allowed = jnp.concatenate([seg_k, seg_k], 1) == seg_q
            if n == TILES - 1:
                allowed = allowed & causal
            s = jnp.where(allowed, s, NEGATIVE)
            s_scr[n * TILE : (n + 1) * TILE, :] = s
            here = fold(s, jnp.maximum)
            peak = here if peak is None else jnp.maximum(peak, here)
        peak = jnp.max(peak, axis=0, keepdims=True) * EXP_SCALE

        total = None
        for n in range(TILES):
            p = jnp.exp2(s_scr[n * TILE : (n + 1) * TILE, :] * EXP_SCALE - peak)
            p_scr[n * TILE : (n + 1) * TILE, :] = p.astype(jnp.bfloat16)
            here = fold(p, jnp.add)
            total = here if total is None else total + here
        inverse = 1.0 / jnp.sum(total, axis=0, keepdims=True)

        window = pl.ds(base, WIN)
        attended = dot(kvt[1, :, window], p_scr[...]) * inverse
        gst = gs.astype(jnp.float32).T * inverse
        gst = gst.astype(jnp.bfloat16)
        delta = jnp.sum(gst.astype(jnp.float32) * attended, axis=0, keepdims=True)
        rows = pl.ds(pl.multiple_of(j * SUB, SUB), SUB)

        def store(ref, value):
            value = value.T.astype(jnp.bfloat16)
            for h in range(GROUP):
                ref[rows, h * HD : (h + 1) * HD] = value[h * SUB : (h + 1) * SUB]

        store(out_ref, attended)
        for n in range(TILES):
            p = p_scr[n * TILE : (n + 1) * TILE, :]
            slope = dot(kv[1, keys(n), :], gst)
            e = (p.astype(jnp.float32) * (slope - delta)).astype(jnp.bfloat16)
            e_scr[n * TILE : (n + 1) * TILE, :] = e
            acc[0, keys(n), :] += dot(e, qs)
            acc[1, keys(n), :] += dot_nt(p, gst)
        store(dq_ref, dot(kvt[0, :, window], e_scr[...]) * SCALING)
        return carry

    lax.fori_loop(0, TP, unit, 0)

    def term_copy(d):
        return pltpu.make_async_remote_copy(
            src_ref=tx.at[d - 1],
            dst_ref=rx.at[d - 1],
            send_sem=t_send.at[d - 1],
            recv_sem=t_recv.at[d - 1],
            device_id={"ctx": (c + CTX - d) % CTX},
            device_id_type=MESH,
        )

    for d in (2, 1):
        at = (2 - d) * TOK
        tx[d - 1, 0] = (acc[0, at : at + TOK, :] * SCALING).astype(jnp.bfloat16)
        tx[d - 1, 1] = acc[1, at : at + TOK, :].astype(jnp.bfloat16)

        @pl.when(c >= d)
        def _():
            term_copy(d).start()

    for d in (2, 1):

        @pl.when(c < CTX - d)
        def _():
            term_copy(d).wait_recv()

        @pl.when(c >= CTX - d)
        def _():
            rx[d - 1] = jnp.zeros((2, TOK, HD), jnp.bfloat16)

    for w, ref in ((0, dk_ref), (1, dv_ref)):
        own_sum = acc[w, 2 * TOK : 3 * TOK, :]
        if w == 0:
            own_sum = own_sum * SCALING
        ref[...] = (
            own_sum + rx[0, w].astype(jnp.float32) + rx[1, w].astype(jnp.float32)
        ).astype(jnp.bfloat16)

    for dz, dc in partners:
        for copy in key_copies(partner(dz, dc)) + query_copies(partner(dz, dc)):
            copy.wait_send()
    for d in (1, 2):

        @pl.when(c < CTX - d)
        def _():
            window_copy(d).wait_send()

        @pl.when(c >= d)
        def _():
            term_copy(d).wait_send()


def on_device(query, key_states, value_states, grad_out, segment_ids):
    vmem = pl.BlockSpec(memory_space=pltpu.VMEM)
    hbm = pl.BlockSpec(memory_space=pl.ANY)
    bf16, f32 = jnp.bfloat16, jnp.float32
    dma = pltpu.SemaphoreType.DMA
    return pl.pallas_call(
        kernel,
        out_shape=(
            jax.ShapeDtypeStruct((TOK, GROUP * HD), bf16),
            jax.ShapeDtypeStruct((TOK, GROUP * HD), bf16),
            jax.ShapeDtypeStruct((TOK, HD), bf16),
            jax.ShapeDtypeStruct((TOK, HD), bf16),
        ),
        in_specs=[hbm, hbm, hbm, hbm, vmem],
        out_specs=(vmem, vmem, vmem, vmem),
        scratch_shapes=[
            pltpu.VMEM((TP, SUB, GROUP * HD), bf16),
            pltpu.VMEM((TP, SUB, GROUP * HD), bf16),
            pltpu.VMEM((2, 3 * TOK, HD), bf16),
            pltpu.VMEM((2, HD, 3 * TOK), bf16),
            pltpu.VMEM((3 * TOK, TILE), f32),
            pltpu.VMEM((TP, 8, LANES), f32),
            pltpu.VMEM((WIN, LANES), f32),
            pltpu.VMEM((WIN, LANES), bf16),
            pltpu.VMEM((WIN, LANES), bf16),
            pltpu.VMEM((2, 3 * TOK, HD), f32),
            pltpu.VMEM((2, 2, TOK, HD), bf16),
            pltpu.VMEM((2, 2, TOK, HD), bf16),
        ]
        + [dma((TP,))] * 8
        + [dma((2,))] * 4,
        compiler_params=pltpu.CompilerParams(
            collective_id=0, has_side_effects=True, vmem_limit_bytes=32 * 2**20
        ),
        cost_estimate=pl.CostEstimate(
            flops=2 * 6 * TP * LANES * WIN * HD,
            bytes_accessed=4 * TOK * GROUP * HD * 2,
            transcendentals=TP * LANES * WIN,
        ),
        name="attention",
    )(query, key_states, value_states, grad_out, segment_ids.reshape(-1, TILE))


def solution(mesh):
    in_specs = (
        P(("ctx", "tp"), None),
        P(("ctx", "tp"), None),
        P(("ctx", "tp"), None),
        P(("ctx", "tp"), None),
        P(),
    )
    out_specs = (P("ctx", "tp"), P("ctx", "tp"), P("ctx", "tp"), P("ctx", "tp"))
    return jax.shard_map(
        on_device, mesh=mesh, in_specs=in_specs, out_specs=out_specs, check_vma=False
    )
```

time: 257 us -> 135 us (0.53)
  the two profiles are of different devices: /device:TPU:40 before, /device:TPU:30 now
where the time goes in v1:
time: 135 us
  Pallas kernels  126 us (93%)
  local copies, waits for them, and re-layouts  7.68 us (6%)
    pallas_call x1, Pallas kernels, on_device(): pl.pallas_call(kernel, out_shape=(jax.ShapeDtypeStruct((TOK, GROUP * HD),...  126 us
    unnamed x14, local copies, waits for them, and re-layouts  7.68 us

profile of v1, /device:TPU:30, one launch (start us, length us, event | category | flops | bytes accessed | tf_op | source)
XLA Modules:
  0.0 134.5 jit_solution(4707696968387164511)
XLA Ops:
  0.6 0.0 copy-start
  0.6 1.0 copy-done
  1.7 0.0 copy-start.1
  1.7 1.0 copy-done.1
  2.7 0.0 copy-start.2
  2.7 0.9 copy-done.2
  3.6 0.0 copy-start.3
  3.6 0.9 copy-done.3
  4.5 0.0 copy-start.4
  4.5 0.9 copy-done.4
  5.4 126.2 %attention.1 = (bf16[512,512]{1,0:T(8,128)(2,1)S(1)}, bf16[512,512]{1,0:T(8,128)(2,1)S(1)}, bf16[512,128]{1,0:T(8,128)(2,1)S(1)}, bf16[512,128]{1,0:T(8,128)(2,1)S(1)}) custom-call(bf16[64,4096]{1,0:T(8,128)(2,1)S(1)} %copy-done, bf16[64,1024]{1,0:T(8,128)(2,1)S(1)} %copy-done.2, bf16[64,1024]{1,0:T(8,128)(2,1)S(1)} %copy-done.3, ...), custom_call_target="tpu_custom_call" | custom-call | flops 3623878656 | bytes 2097152 | tf_op jit(solution)/shard_map/attention/pallas_call | solution.py:329
  131.6 0.8 copy.13
  132.4 0.8 copy.14
  133.2 0.7 copy.15
  133.9 0.7 copy.16
Async XLA Ops:
  0.6 1.0 copy-start
  1.7 1.0 copy-start.1
  2.7 0.9 copy-start.2
  3.6 0.9 copy-start.3
  4.5 0.9 copy-start.4

commit v2 on v1

v2 whole, which is shorter than its diff:
```python
import math

import jax
import jax.numpy as jnp
from jax import lax
from jax.experimental import pallas as pl
from jax.experimental.pallas import tpu as pltpu
from jax.sharding import PartitionSpec as P

QH = 32
KVH = 8
HD = 128
TOK = 512
SUB = 64
GROUP = QH // KVH
CTX = 64
PLANE = 16
PLANES = CTX // PLANE
EARLY = 2
TP = 8
LANES = SUB * GROUP
WIN = 1152
TILE = 128
TILES = WIN // TILE
NEGATIVE = -1e30
MESH = pl.DeviceIdType.MESH
SCALING = HD**-0.5
EXP_SCALE = SCALING * math.log2(math.e)

PARTS = ((2, 0, TOK // 2), (2, TOK // 2, TOK // 2), (1, TOK, TOK))

NT = (((1,), (1,)), ((), ()))


def dot(a, b):
    return jnp.dot(a, b, preferred_element_type=jnp.float32)


def dot_nt(a, b):
    return lax.dot_general(a, b, NT, preferred_element_type=jnp.float32)


def fold(x, op):
    parts = [x[i * 8 : (i + 1) * 8] for i in range(x.shape[0] // 8)]
    while len(parts) > 1:
        parts = [op(parts[i], parts[i + 1]) for i in range(0, len(parts), 2)]
    return parts[0]


def kernel(
    q_in,
    k_in,
    v_in,
    g_in,
    seg_in,
    out_ref,
    dq_ref,
    dk_ref,
    dv_ref,
    q_vm,
    g_vm,
    k_vm,
    v_vm,
    kv_out,
    qg_out,
    qg,
    kv,
    kvt,
    segcol,
    segrow,
    s_scr,
    p_scr,
    e_scr,
    acc,
    tx,
    rx,
    load_sem,
    q_send,
    q_recv,
    k_send,
    k_recv,
    w_send,
    w_recv,
    t_send,
    t_recv,
    seg,
    relay,
    seg_sem,
    r_send,
    r_recv,
    x_send,
    x_recv,
):
    c = lax.axis_index("ctx")
    t = lax.axis_index("tp")
    zh, co = t // 2, t % 2
    plane, p = c // PLANE, c % PLANE

    seg_copy = pltpu.make_async_copy(seg_in, seg, seg_sem)
    seg_copy.start()
    loads = [
        pltpu.make_async_copy(k_in, k_vm, load_sem.at[0]),
        pltpu.make_async_copy(v_in, v_vm, load_sem.at[1]),
        pltpu.make_async_copy(q_in, q_vm, load_sem.at[2]),
        pltpu.make_async_copy(g_in, g_vm, load_sem.at[3]),
    ]
    for load in loads:
        load.start()

    barrier = pltpu.get_barrier_semaphore()
    for d in range(1, TP):
        pl.semaphore_signal(barrier, inc=1, device_id={"tp": (t + d) % TP}, device_id_type=MESH)
    for d in (1, 2, CTX - 1, CTX - 2):
        pl.semaphore_signal(barrier, inc=1, device_id={"ctx": (c + d) % CTX}, device_id_type=MESH)

    crossing = plane < PLANES - 1

    def greet(block, to=t):
        pl.semaphore_signal(
            barrier, inc=1, device_id={"ctx": block, "tp": to}, device_id_type=MESH
        )

    first = plane * PLANE

    @pl.when(p < 8)
    def _():
        greet(first + 15)

    @pl.when((p >= 8) & (p != 14))
    def _():
        greet(first + 14)

    @pl.when(p == 15)
    def _():
        for r in range(TP):
            greet(first + r)

    @pl.when(p == 14)
    def _():
        for r in range(TP):
            if r != 6:
                greet(first + 8 + r)

    @pl.when((p == 0) & (plane >= 1))
    def _():
        for r in range(TP):
            greet(first - PLANE + t, r)
            greet(first - PLANE + 8 + t, r)

    arrivals = (
        TP - 1 + 4 + jnp.where(p < 14, 1, jnp.where(p == 14, 7, 9)) + jnp.where(crossing, 1, 0)
    )

    def own_rows(j):
        return pl.ds(pl.multiple_of(2 * TOK + j * SUB, SUB), SUB)

    for load in loads:
        load.wait()
    for j in range(TP):
        kv_out[j, 0] = k_vm[:, j * HD : (j + 1) * HD]
        kv_out[j, 1] = v_vm[:, j * HD : (j + 1) * HD]
    for j in range(TP):
        for h in range(GROUP):
            at = (j * GROUP + h) * HD
            qg_out[j, h] = q_vm[:, at : at + HD]
            qg_out[j, GROUP + h] = g_vm[:, at : at + HD]

    @pl.when(c < 1)
    def _():
        kv[:, TOK : 2 * TOK] = jnp.zeros((2, TOK, HD), jnp.bfloat16)

    @pl.when(c < 2)
    def _():
        kv[:, 0:TOK] = jnp.zeros((2, TOK, HD), jnp.bfloat16)

    kv[:, own_rows(t), :] = kv_out[t]
    qg[t] = qg_out[t]
    acc[...] = jnp.zeros_like(acc)

    seg_copy.wait()
    for block in range(3):
        at = jnp.maximum(c - 2 + block, 0)
        rows = seg[pl.ds(pl.multiple_of(at * 4, 4), 4), :].astype(jnp.float32)
        rows = jnp.where(c - 2 + block >= 0, rows, -1.0)
        for i in range(4):
            wide_row = jnp.broadcast_to(rows[i : i + 1], (TILE, TILE))
            start = block * TOK + i * TILE
            segcol[start : start + TILE, :] = wide_row.T
    own = seg[pl.ds(pl.multiple_of(c * 4, 4), 4), :].astype(jnp.float32)
    low_lane = lax.broadcasted_iota(jnp.int32, (8, TILE), 1) < SUB
    for i in range(4):
        row = jnp.broadcast_to(own[i : i + 1], (8, TILE))
        turned = pltpu.roll(row, SUB, 1)
        low = jnp.where(low_lane, row, turned)
        high = jnp.where(low_lane, turned, row)
        segrow[2 * i] = jnp.concatenate([low, low], 1)
        segrow[2 * i + 1] = jnp.concatenate([high, high], 1)

    pl.semaphore_wait(barrier, arrivals)

    def partner(dz, dc):
        return ((zh + dz) % 4) * 2 + (co + dc) % 2

    partners = [(1, 0), (3, 0), (1, 1), (3, 1), (2, 0), (2, 1), (0, 1)]
    to_1, to_2, to_3 = (zh + 1) % 4, (zh + 3) % 4, (zh + 2) % 4
    targets = [to_1 * 2 + co, to_2 * 2 + co, to_1 * 2 + 1 - co, to_2 * 2 + 1 - co]
    targets += [zh * 2 + 1 - co, to_3 * 2 + co, to_3 * 2 + 1 - co]

    def exchange(src, dst, send, recv, to):
        return pltpu.make_async_remote_copy(
            src_ref=src,
            dst_ref=dst,
            send_sem=send.at[to],
            recv_sem=recv.at[t],
            device_id={"tp": to},
            device_id_type=MESH,
        )

    def key_copy(to):
        return exchange(kv_out.at[to], kv.at[:, own_rows(t)], k_send, k_recv, to)

    def query_copy(to):
        return exchange(qg_out.at[to], qg.at[t], q_send, q_recv, to)

    def relay_copy(r):
        return pltpu.make_async_remote_copy(
            src_ref=kv_out.at[r],
            dst_ref=relay,
            send_sem=r_send.at[r],
            recv_sem=r_recv,
            device_id={"ctx": first + r + 8 * (15 - p)},
            device_id_type=MESH,
        )

    def cross_copy(src):
        at = jnp.where(p < 8, TOK, 0) + t * SUB
        return pltpu.make_async_remote_copy(
            src_ref=src,
            dst_ref=kv.at[:, pl.ds(pl.multiple_of(at, SUB), SUB)],
            send_sem=x_send,
            recv_sem=x_recv.at[jnp.where(p < 8, 0, 8) + t],
            device_id={"ctx": (plane + 1) % PLANES * PLANE, "tp": p % 8},
            device_id_type=MESH,
        )

    @pl.when((p == 15) & crossing)
    def _():
        for r in range(TP):
            relay_copy(r).start()

    @pl.when((p == 14) & crossing)
    def _():
        for r in range(TP):
            if r != 6:
                relay_copy(r).start()
        cross_copy(kv_out.at[6]).start()

    for dz, dc in partners:
        key_copy(partner(dz, dc)).start()

    @pl.when((p != 14) & crossing)
    def _():
        pltpu.make_async_copy(relay, relay, r_recv).wait()
        cross_copy(relay).start()

    for to in targets[:EARLY]:
        query_copy(to).start()

    for dz, dc in partners:
        j = partner(dz, dc)
        rows = kv.at[:, own_rows(j)]
        pltpu.make_async_copy(rows, rows, k_recv.at[j]).wait()

    def window_copy(d):
        return pltpu.make_async_remote_copy(
            src_ref=kv.at[:, pl.ds(2 * TOK, TOK)],
            dst_ref=kv.at[:, pl.ds((2 - d) * TOK, TOK)],
            send_sem=w_send.at[d - 1],
            recv_sem=w_recv.at[d - 1],
            device_id={"ctx": (c + d) % CTX},
            device_id_type=MESH,
        )

    def wait_cross(column):
        chunk = kv.at[:, pl.ds(0, SUB)]
        pltpu.make_async_copy(chunk, chunk, x_recv.at[column]).wait()

    def onward_copy():
        return pltpu.make_async_remote_copy(
            src_ref=kv.at[:, pl.ds(TOK, TOK)],
            dst_ref=kv.at[:, pl.ds(0, TOK)],
            send_sem=w_send.at[1],
            recv_sem=w_recv.at[1],
            device_id={"ctx": (c + 1) % CTX},
            device_id_type=MESH,
        )

    for d in (1, 2):

        @pl.when(p < PLANE - d)
        def _():
            window_copy(d).start()

    def turn(start):
        for i in range(TOK // TILE):
            at = start + i * TILE
            for w in range(2):
                block = kv[w, at : at + TILE, :].astype(jnp.float32)
                kvt[w, :, at : at + TILE] = block.T.astype(jnp.bfloat16)

    turn(2 * TOK)

    @pl.when((p == 0) & (plane >= 1))
    def _():
        for column in range(8):
            wait_cross(column)
        onward_copy().start()
        for column in range(8, 16):
            wait_cross(column)

    for d in (1, 2):

        @pl.when((p >= 1) & (c >= d))
        def _():
            window_copy(d).wait_recv()

        if d == 2:
            for to in targets[EARLY:]:
                query_copy(to).start()
        turn((2 - d) * TOK)

    lane = lax.broadcasted_iota(jnp.int32, (TILE, LANES), 1) % SUB
    place = lax.broadcasted_iota(jnp.int32, (TILE, LANES), 0)

    def term_copy(part):
        d, start, size = PARTS[part]
        return pltpu.make_async_remote_copy(
            src_ref=tx.at[:, pl.ds(start, size)],
            dst_ref=rx.at[:, pl.ds(start, size)],
            send_sem=t_send.at[part],
            recv_sem=t_recv.at[part],
            device_id={"ctx": (c + CTX - d) % CTX},
            device_id_type=MESH,
        )

    def send_terms(part):
        d, start, size = PARTS[part]
        tx[0, start : start + size] = (acc[0, start : start + size] * SCALING).astype(jnp.bfloat16)
        tx[1, start : start + size] = acc[1, start : start + size].astype(jnp.bfloat16)

        @pl.when(c >= d)
        def _():
            term_copy(part).start()

    early_half = zh < 2

    def unit(i, final):
        a = i // 2
        dz = a + a // 2 - 2 * (a // 3)
        sz, sc = (zh + dz) % 4, (co + i) % 2
        j = sz * 2 + sc

        def arrived():
            pltpu.make_async_copy(qg.at[j], qg.at[j], q_recv.at[j]).wait()

        if final:
            arrived()
        else:
            pl.when(i > 0)(arrived)
        base = pl.multiple_of(sz * TILE, TILE)

        def keys(n):
            return pl.ds(pl.multiple_of(base + n * TILE, TILE), TILE)

        qs = qg[j, :GROUP].reshape(LANES, HD)
        gs = qg[j, GROUP:].reshape(LANES, HD)
        seg_q = segrow[j][0:1]
        causal = place <= lane + sc * SUB

        peak = None
        for n in range(TILES):
            s = dot_nt(kv[0, keys(n), :], qs)
            seg_k = segcol[keys(n), :]
            allowed = jnp.concatenate([seg_k, seg_k], 1) == seg_q
            if n == TILES - 1:
                allowed = allowed & causal
            s = jnp.where(allowed, s, NEGATIVE)
            s_scr[n * TILE : (n + 1) * TILE, :] = s
            here = fold(s, jnp.maximum)
            peak = here if peak is None else jnp.maximum(peak, here)
        peak = jnp.max(peak, axis=0, keepdims=True) * EXP_SCALE

        total = None
        for n in range(TILES):
            p = jnp.exp2(s_scr[n * TILE : (n + 1) * TILE, :] * EXP_SCALE - peak)
            p_scr[n * TILE : (n + 1) * TILE, :] = p.astype(jnp.bfloat16)
            here = fold(p, jnp.add)
            total = here if total is None else total + here
        inverse = 1.0 / jnp.sum(total, axis=0, keepdims=True)

        window = pl.ds(base, WIN)
        attended = dot(kvt[1, :, window], p_scr[...]) * inverse
        gst = gs.astype(jnp.float32).T * inverse
        gst = gst.astype(jnp.bfloat16)
        delta = jnp.sum(gst.astype(jnp.float32) * attended, axis=0, keepdims=True)
        rows = pl.ds(pl.multiple_of(j * SUB, SUB), SUB)

        def store(ref, value):
            value = value.T.astype(jnp.bfloat16)
            for h in range(GROUP):
                ref[rows, h * HD : (h + 1) * HD] = value[h * SUB : (h + 1) * SUB]

        for n in range(TILES):
            p = p_scr[n * TILE : (n + 1) * TILE, :]
            slope = dot(kv[1, keys(n), :], gst)
            e = (p.astype(jnp.float32) * (slope - delta)).astype(jnp.bfloat16)
            e_scr[n * TILE : (n + 1) * TILE, :] = e
            acc[0, keys(n), :] += dot(e, qs)
            acc[1, keys(n), :] += dot_nt(p, gst)
            if final and n == 3:

                @pl.when(jnp.logical_not(early_half))
                def _():
                    send_terms(0)

                send_terms(1)
            if final and n == 7:
                send_terms(2)
        store(out_ref, attended)
        store(dq_ref, dot(kvt[0, :, window], e_scr[...]) * SCALING)

    def one_unit(i, carry):
        unit(i, False)

        @pl.when((i == TP - 3) & early_half)
        def _():
            send_terms(0)

        return carry

    lax.fori_loop(0, TP - 1, one_unit, 0)
    unit(TP - 1, True)

    for part, (d, start, size) in enumerate(PARTS):

        @pl.when(c < CTX - d)
        def _():
            term_copy(part).wait_recv()

        @pl.when(c >= CTX - d)
        def _():
            rx[:, start : start + size] = jnp.zeros((2, size, HD), jnp.bfloat16)

    for w, ref in ((0, dk_ref), (1, dv_ref)):
        own_sum = acc[w, 2 * TOK : 3 * TOK, :]
        if w == 0:
            own_sum = own_sum * SCALING
        far = rx[w, 0:TOK].astype(jnp.float32)
        near = rx[w, TOK : 2 * TOK].astype(jnp.float32)
        ref[...] = (own_sum + near + far).astype(jnp.bfloat16)

    for dz, dc in partners:
        key_copy(partner(dz, dc)).wait_send()
        query_copy(partner(dz, dc)).wait_send()
    @pl.when((p >= 14) & crossing)
    def _():
        for r in range(TP):
            if r != 6:
                relay_copy(r).wait_send()

    @pl.when((p == 15) & crossing)
    def _():
        relay_copy(6).wait_send()

    @pl.when(crossing)
    def _():
        cross_copy(relay).wait_send()

    @pl.when((p == 0) & (plane >= 1))
    def _():
        onward_copy().wait_send()

    for d in (1, 2):

        @pl.when(p < PLANE - d)
        def _():
            window_copy(d).wait_send()

    for part, (d, start, size) in enumerate(PARTS):

        @pl.when(c >= d)
        def _():
            term_copy(part).wait_send()


def hand_over(*refs):
    sources, results, held, come, gone = refs[:4], refs[4:8], refs[8:12], refs[12], refs[13]
    ins = [pltpu.make_async_copy(sources[i], held[i], come.at[i]) for i in range(4)]
    outs = [pltpu.make_async_copy(held[i], results[i], gone.at[i]) for i in range(4)]
    for copy in ins:
        copy.start()
    for copy, onward in zip(ins, outs):
        copy.wait()
        onward.start()
    for onward in outs:
        onward.wait()


def on_device(query, key_states, value_states, grad_out, segment_ids):
    vmem = pl.BlockSpec(memory_space=pltpu.VMEM)
    hbm = pl.BlockSpec(memory_space=pltpu.HBM)
    bf16, f32 = jnp.bfloat16, jnp.float32
    dma = pltpu.SemaphoreType.DMA
    shapes = (
            jax.ShapeDtypeStruct((TOK, GROUP * HD), bf16),
            jax.ShapeDtypeStruct((TOK, GROUP * HD), bf16),
            jax.ShapeDtypeStruct((TOK, HD), bf16),
            jax.ShapeDtypeStruct((TOK, HD), bf16),
    )
    results = pl.pallas_call(
        kernel,
        out_shape=shapes,
        in_specs=[hbm, hbm, hbm, hbm, hbm],
        out_specs=(vmem, vmem, vmem, vmem),
        scratch_shapes=[
            pltpu.VMEM((SUB, QH * HD), bf16),
            pltpu.VMEM((SUB, QH * HD), bf16),
            pltpu.VMEM((SUB, KVH * HD), bf16),
            pltpu.VMEM((SUB, KVH * HD), bf16),
            pltpu.VMEM((TP, 2, SUB, HD), bf16),
            pltpu.VMEM((TP, 2 * GROUP, SUB, HD), bf16),
            pltpu.VMEM((TP, 2 * GROUP, SUB, HD), bf16),
            pltpu.VMEM((2, 3 * TOK, HD), bf16),
            pltpu.VMEM((2, HD, 3 * TOK), bf16),
            pltpu.VMEM((3 * TOK, TILE), f32),
            pltpu.VMEM((TP, 8, LANES), f32),
            pltpu.VMEM((WIN, LANES), f32),
            pltpu.VMEM((WIN, LANES), bf16),
            pltpu.VMEM((WIN, LANES), bf16),
            pltpu.VMEM((2, 3 * TOK, HD), f32),
            pltpu.VMEM((2, 2 * TOK, HD), bf16),
            pltpu.VMEM((2, 2 * TOK, HD), bf16),
        ]
        + [dma((4,))]
        + [dma((TP,))] * 4
        + [dma((2,))] * 2
        + [dma((3,))] * 2
        + [
            pltpu.VMEM((CTX * TOK // TILE, TILE), jnp.int32),
            pltpu.VMEM((2, SUB, HD), bf16),
            dma,
            dma((TP,)),
            dma,
            dma,
            dma((PLANE,)),
        ],
        compiler_params=pltpu.CompilerParams(
            collective_id=0, has_side_effects=True, vmem_limit_bytes=56 * 2**20
        ),
        cost_estimate=pl.CostEstimate(
            flops=2 * 6 * TP * LANES * WIN * HD,
            bytes_accessed=4 * TOK * GROUP * HD * 2,
            transcendentals=TP * LANES * WIN,
        ),
        name="attention",
    )(query, key_states, value_states, grad_out, segment_ids.reshape(-1, TILE))
    whole = pl.BlockSpec(memory_space=pl.ANY)
    return pl.pallas_call(
        hand_over,
        out_shape=shapes,
        in_specs=[whole] * 4,
        out_specs=(whole,) * 4,
        scratch_shapes=[pltpu.VMEM(shape.shape, shape.dtype) for shape in shapes]
        + [dma((4,)), dma((4,))],
        compiler_params=pltpu.CompilerParams(vmem_limit_bytes=56 * 2**20),
        name="hand_over",
    )(*results)


def solution(mesh):
    in_specs = (
        P(("ctx", "tp"), None),
        P(("ctx", "tp"), None),
        P(("ctx", "tp"), None),
        P(("ctx", "tp"), None),
        P(),
    )
    out_specs = (P("ctx", "tp"), P("ctx", "tp"), P("ctx", "tp"), P("ctx", "tp"))
    return jax.shard_map(
        on_device, mesh=mesh, in_specs=in_specs, out_specs=out_specs, check_vma=False
    )
```

time: 135 us -> 106 us (0.79)
  the two profiles are of different devices: /device:TPU:30 before, /device:TPU:16 now
where the time goes in v2:
time: 106 us
  Pallas kernels  105 us (99%)
    pallas_call x1, Pallas kernels, on_device(): pl.pallas_call(kernel, out_shape=shapes, in_specs=[hbm, hbm, hbm, hbm, hb...  103 us
    pallas_call x1, Pallas kernels, on_device(): pl.pallas_call(hand_over, out_shape=shapes, in_specs=[whole] * 4, out_spe...  2.15 us

profile of v2, /device:TPU:16, one launch (start us, length us, event | category | flops | bytes accessed | tf_op | source)
XLA Modules:
  0.0 106.0 jit_solution(130759329202873271)
XLA Ops:
  0.6 103.2 %attention.1 = (bf16[512,512]{1,0:T(8,128)(2,1)}, bf16[512,512]{1,0:T(8,128)(2,1)}, bf16[512,128]{1,0:T(8,128)(2,1)}, bf16[512,128]{1,0:T(8,128)(2,1)}) custom-call(bf16[64,4096]{1,0:T(8,128)(2,1)} %q_in.1, bf16[64,1024]{1,0:T(8,128)(2,1)} %k_in.1, bf16[64,1024]{1,0:T(8,128)(2,1)} %v_in.1, bf16[64,4096]{1,0:T(8,128)(2,1)} %g_in.1, s32[256,128]{1,0:T(8,128)} %bitcast.1), custom_call_target="tpu_custom_call" | custom-call | flops 3623878656 | bytes 2097152 | tf_op jit(solution)/shard_map/attention/pallas_call | solution.py:520
  103.8 2.2 %hand_over.1 = (bf16[512,512]{1,0:T(8,128)(2,1)}, bf16[512,512]{1,0:T(8,128)(2,1)}, bf16[512,128]{1,0:T(8,128)(2,1)}, bf16[512,128]{1,0:T(8,128)(2,1)}) custom-call(bf16[512,512]{1,0:T(8,128)(2,1)} %get-tuple-element.8.refs_0_, bf16[512,512]{1,0:T(8,128)(2,1)} %get-tuple-element.9.refs_1_, bf16[512,128]{1,0:T(8,128)(2,1)} %get-tuple-element.10.refs_2_, ...), custom_call_target="tpu_custom_call" | custom-call | tf_op jit(solution)/shard_map/hand_over/pallas_call | solution.py:568

commit v3 on v2

--- a/solution.py
+++ b/solution.py
@@ -16,9 +16,11 @@
 CTX = 64
 PLANE = 16
 PLANES = CTX // PLANE
-EARLY = 2
+EARLY = 3
 TP = 8
-LANES = SUB * GROUP
+HALF = SUB * GROUP
+LANES = 2 * HALF
+UNITS = TP // 2
 WIN = 1152
 TILE = 128
 TILES = WIN // TILE
@@ -27,7 +29,7 @@
 SCALING = HD**-0.5
 EXP_SCALE = SCALING * math.log2(math.e)
 
-PARTS = ((2, 0, TOK // 2), (2, TOK // 2, TOK // 2), (1, TOK, TOK))
+PARTS = ((2, 0, 256), (2, 256, 256), (1, 512, 256), (1, 768, 256))
 
 NT = (((1,), (1,)), ((), ()))
 
@@ -71,6 +73,7 @@
     s_scr,
     p_scr,
     e_scr,
+    gst_scr,
     acc,
     tx,
     rx,
@@ -203,8 +206,8 @@
 
     partners = [(1, 0), (3, 0), (1, 1), (3, 1), (2, 0), (2, 1), (0, 1)]
     to_1, to_2, to_3 = (zh + 1) % 4, (zh + 3) % 4, (zh + 2) % 4
-    targets = [to_1 * 2 + co, to_2 * 2 + co, to_1 * 2 + 1 - co, to_2 * 2 + 1 - co]
-    targets += [zh * 2 + 1 - co, to_3 * 2 + co, to_3 * 2 + 1 - co]
+    targets = [zh * 2 + 1 - co, to_1 * 2 + co, to_2 * 2 + co]
+    targets += [to_1 * 2 + 1 - co, to_2 * 2 + 1 - co, to_3 * 2 + co, to_3 * 2 + 1 - co]
 
     def exchange(src, dst, send, recv, to):
         return pltpu.make_async_remote_copy(
@@ -266,21 +269,33 @@
     for to in targets[:EARLY]:
         query_copy(to).start()
 
-    for dz, dc in partners:
-        j = partner(dz, dc)
-        rows = kv.at[:, own_rows(j)]
-        pltpu.make_async_copy(rows, rows, k_recv.at[j]).wait()
-
-    def window_copy(d):
+    def window_copy(d, j):
         return pltpu.make_async_remote_copy(
-            src_ref=kv.at[:, pl.ds(2 * TOK, TOK)],
-            dst_ref=kv.at[:, pl.ds((2 - d) * TOK, TOK)],
+            src_ref=kv.at[:, own_rows(j)],
+            dst_ref=kv.at[:, pl.ds(pl.multiple_of((2 - d) * TOK + j * SUB, SUB), SUB)],
             send_sem=w_send.at[d - 1],
             recv_sem=w_recv.at[d - 1],
             device_id={"ctx": (c + d) % CTX},
             device_id_type=MESH,
         )
 
+    def wait_window(sem):
+        pltpu.make_async_copy(kv.at[:, pl.ds(0, TOK)], kv.at[:, pl.ds(0, TOK)], sem).wait()
+
+    def send_window(j):
+        for d in (1, 2):
+
+            @pl.when(p < PLANE - d)
+            def _():
+                window_copy(d, j).start()
+
+    send_window(t)
+    for dz, dc in [(0, 1)] + partners[:-1]:
+        j = partner(dz, dc)
+        rows = kv.at[:, own_rows(j)]
+        pltpu.make_async_copy(rows, rows, k_recv.at[j]).wait()
+        send_window(j)
+
     def wait_cross(column):
         chunk = kv.at[:, pl.ds(0, SUB)]
         pltpu.make_async_copy(chunk, chunk, x_recv.at[column]).wait()
@@ -289,17 +304,11 @@
         return pltpu.make_async_remote_copy(
             src_ref=kv.at[:, pl.ds(TOK, TOK)],
             dst_ref=kv.at[:, pl.ds(0, TOK)],
-            send_sem=w_send.at[1],
+            send_sem=w_send.at[2],
             recv_sem=w_recv.at[1],
             device_id={"ctx": (c + 1) % CTX},
             device_id_type=MESH,
         )
-
-    for d in (1, 2):
-
-        @pl.when(p < PLANE - d)
-        def _():
-            window_copy(d).start()
 
     def turn(start):
         for i in range(TOK // TILE):
@@ -322,15 +331,15 @@
 
         @pl.when((p >= 1) & (c >= d))
         def _():
-            window_copy(d).wait_recv()
+            wait_window(w_recv.at[d - 1])
 
         if d == 2:
             for to in targets[EARLY:]:
                 query_copy(to).start()
         turn((2 - d) * TOK)
 
-    lane = lax.broadcasted_iota(jnp.int32, (TILE, LANES), 1) % SUB
-    place = lax.broadcasted_iota(jnp.int32, (TILE, LANES), 0)
+    lane = lax.broadcasted_iota(jnp.int32, (TILE, HALF), 1) % SUB
+    place = lax.broadcasted_iota(jnp.int32, (TILE, HALF), 0)
 
     def term_copy(part):
         d, start, size = PARTS[part]
@@ -355,91 +364,99 @@
     early_half = zh < 2
 
     def unit(i, final):
-        a = i // 2
-        dz = a + a // 2 - 2 * (a // 3)
-        sz, sc = (zh + dz) % 4, (co + i) % 2
-        j = sz * 2 + sc
-
-        def arrived():
+        dz = i + i // 2 - 2 * (i // 3)
+        sz = (zh + dz) % 4
+
+        def arrived(j):
             pltpu.make_async_copy(qg.at[j], qg.at[j], q_recv.at[j]).wait()
 
         if final:
-            arrived()
+            arrived(sz * 2 + co)
         else:
-            pl.when(i > 0)(arrived)
+            pl.when(i > 0)(lambda: arrived(sz * 2 + co))
+        arrived(sz * 2 + 1 - co)
         base = pl.multiple_of(sz * TILE, TILE)
+        window = pl.ds(base, WIN)
+        halves = [slice(0, HALF), slice(HALF, LANES)]
 
         def keys(n):
             return pl.ds(pl.multiple_of(base + n * TILE, TILE), TILE)
 
-        qs = qg[j, :GROUP].reshape(LANES, HD)
-        gs = qg[j, GROUP:].reshape(LANES, HD)
-        seg_q = segrow[j][0:1]
-        causal = place <= lane + sc * SUB
-
-        peak = None
-        for n in range(TILES):
-            s = dot_nt(kv[0, keys(n), :], qs)
-            seg_k = segcol[keys(n), :]
-            allowed = jnp.concatenate([seg_k, seg_k], 1) == seg_q
-            if n == TILES - 1:
-                allowed = allowed & causal
-            s = jnp.where(allowed, s, NEGATIVE)
-            s_scr[n * TILE : (n + 1) * TILE, :] = s
-            here = fold(s, jnp.maximum)
-            peak = here if peak is None else jnp.maximum(peak, here)
-        peak = jnp.max(peak, axis=0, keepdims=True) * EXP_SCALE
-
-        total = None
-        for n in range(TILES):
-            p = jnp.exp2(s_scr[n * TILE : (n + 1) * TILE, :] * EXP_SCALE - peak)
-            p_scr[n * TILE : (n + 1) * TILE, :] = p.astype(jnp.bfloat16)
-            here = fold(p, jnp.add)
-            total = here if total is None else total + here
-        inverse = 1.0 / jnp.sum(total, axis=0, keepdims=True)
-
-        window = pl.ds(base, WIN)
-        attended = dot(kvt[1, :, window], p_scr[...]) * inverse
-        gst = gs.astype(jnp.float32).T * inverse
-        gst = gst.astype(jnp.bfloat16)
-        delta = jnp.sum(gst.astype(jnp.float32) * attended, axis=0, keepdims=True)
-        rows = pl.ds(pl.multiple_of(j * SUB, SUB), SUB)
-
-        def store(ref, value):
+        def tile(n):
+            return slice(n * TILE, (n + 1) * TILE)
+
+        both = pl.ds(sz * 2, 2)
+        qs = qg[both, :GROUP].reshape(LANES, HD)
+        gs = qg[both, GROUP:].reshape(LANES, HD)
+
+        terms = []
+        for half, at in enumerate(halves):
+            seg_q = segrow[sz * 2 + half][0:1]
+            causal = place <= lane + half * SUB
+            peak = None
+            for n in range(TILES):
+                s = dot_nt(kv[0, keys(n), :], qs[at])
+                seg_k = segcol[keys(n), :]
+                allowed = jnp.concatenate([seg_k, seg_k], 1) == seg_q
+                if n == TILES - 1:
+                    allowed = allowed & causal
+                s = jnp.where(allowed, s, NEGATIVE)
+                s_scr[tile(n), at] = s
+                here = fold(s, jnp.maximum)
+                peak = here if peak is None else jnp.maximum(peak, here)
+            peak = jnp.max(peak, axis=0, keepdims=True) * EXP_SCALE
+
+            total = None
+            for n in range(TILES):
+                p = jnp.exp2(s_scr[tile(n), at] * EXP_SCALE - peak)
+                p_scr[tile(n), at] = p.astype(jnp.bfloat16)
+                here = fold(p, jnp.add)
+                total = here if total is None else total + here
+            inverse = 1.0 / jnp.sum(total, axis=0, keepdims=True)
+
+            attended = dot(kvt[1, :, window], p_scr[:, at]) * inverse
+            gst = (gs[at].astype(jnp.float32).T * inverse).astype(jnp.bfloat16)
+            delta = jnp.sum(gst.astype(jnp.float32) * attended, axis=0, keepdims=True)
+            gst_scr[:, at] = gst
+            terms.append((attended, gst, delta))
+
+        def store(ref, half, value):
             value = value.T.astype(jnp.bfloat16)
+            rows = pl.ds(pl.multiple_of(base + half * SUB, SUB), SUB)
             for h in range(GROUP):
                 ref[rows, h * HD : (h + 1) * HD] = value[h * SUB : (h + 1) * SUB]
 
         for n in range(TILES):
-            p = p_scr[n * TILE : (n + 1) * TILE, :]
-            slope = dot(kv[1, keys(n), :], gst)
-            e = (p.astype(jnp.float32) * (slope - delta)).astype(jnp.bfloat16)
-            e_scr[n * TILE : (n + 1) * TILE, :] = e
-            acc[0, keys(n), :] += dot(e, qs)
-            acc[1, keys(n), :] += dot_nt(p, gst)
-            if final and n == 3:
+            for half, at in enumerate(halves):
+                attended, gst, delta = terms[half]
+                slope = dot(kv[1, keys(n), :], gst)
+                p = p_scr[tile(n), at].astype(jnp.float32)
+                e_scr[tile(n), at] = (p * (slope - delta)).astype(jnp.bfloat16)
+            acc[0, keys(n), :] += dot(e_scr[tile(n), :], qs)
+            acc[1, keys(n), :] += dot_nt(p_scr[tile(n), :], gst_scr[...])
+            if final and n == 1:
 
                 @pl.when(jnp.logical_not(early_half))
                 def _():
                     send_terms(0)
 
-                send_terms(1)
-            if final and n == 7:
-                send_terms(2)
-        store(out_ref, attended)
-        store(dq_ref, dot(kvt[0, :, window], e_scr[...]) * SCALING)
+            if final and n in (3, 5, 7):
+                send_terms(n // 2)
+        for half, at in enumerate(halves):
+            store(out_ref, half, terms[half][0])
+            store(dq_ref, half, dot(kvt[0, :, window], e_scr[:, at]) * SCALING)
 
     def one_unit(i, carry):
         unit(i, False)
-
-        @pl.when((i == TP - 3) & early_half)
-        def _():
-            send_terms(0)
-
         return carry
 
-    lax.fori_loop(0, TP - 1, one_unit, 0)
-    unit(TP - 1, True)
+    lax.fori_loop(0, UNITS - 1, one_unit, 0)
+
+    @pl.when(early_half)
+    def _():
+        send_terms(0)
+
+    unit(UNITS - 1, True)
 
     for part, (d, start, size) in enumerate(PARTS):
 
@@ -484,7 +501,7 @@
 
         @pl.when(p < PLANE - d)
         def _():
-            window_copy(d).wait_send()
+            wait_window(w_send.at[d - 1])
 
     for part, (d, start, size) in enumerate(PARTS):
 
@@ -533,18 +550,18 @@
             pltpu.VMEM((2, 3 * TOK, HD), bf16),
             pltpu.VMEM((2, HD, 3 * TOK), bf16),
             pltpu.VMEM((3 * TOK, TILE), f32),
-            pltpu.VMEM((TP, 8, LANES), f32),
+            pltpu.VMEM((TP, 8, HALF), f32),
             pltpu.VMEM((WIN, LANES), f32),
             pltpu.VMEM((WIN, LANES), bf16),
             pltpu.VMEM((WIN, LANES), bf16),
+            pltpu.VMEM((HD, LANES), bf16),
             pltpu.VMEM((2, 3 * TOK, HD), f32),
             pltpu.VMEM((2, 2 * TOK, HD), bf16),
             pltpu.VMEM((2, 2 * TOK, HD), bf16),
         ]
         + [dma((4,))]
         + [dma((TP,))] * 4
-        + [dma((2,))] * 2
-        + [dma((3,))] * 2
+        + [dma((3,)), dma((2,)), dma((4,)), dma((4,))]
         + [
             pltpu.VMEM((CTX * TOK // TILE, TILE), jnp.int32),
             pltpu.VMEM((2, SUB, HD), bf16),
@@ -558,9 +575,9 @@
             collective_id=0, has_side_effects=True, vmem_limit_bytes=56 * 2**20
         ),
         cost_estimate=pl.CostEstimate(
-            flops=2 * 6 * TP * LANES * WIN * HD,
+            flops=2 * 6 * UNITS * LANES * WIN * HD,
             bytes_accessed=4 * TOK * GROUP * HD * 2,
-            transcendentals=TP * LANES * WIN,
+            transcendentals=UNITS * LANES * WIN,
         ),
         name="attention",
     )(query, key_states, value_states, grad_out, segment_ids.reshape(-1, TILE))

time: 106 us -> 105 us (level)
  the two profiles are of different devices: /device:TPU:16 before, /device:TPU:15 now
where the time goes in v3:
time: 105 us
  Pallas kernels  104 us (99%)
    pallas_call x1, Pallas kernels, on_device(): pl.pallas_call(kernel, out_shape=shapes, in_specs=[hbm, hbm, hbm, hbm, hb...  102 us
    pallas_call x1, Pallas kernels, on_device(): pl.pallas_call(hand_over, out_shape=shapes, in_specs=[whole] * 4, out_spe...  2.15 us

profile of v3, /device:TPU:15, one launch (start us, length us, event | category | flops | bytes accessed | tf_op | source)
XLA Modules:
  0.0 104.9 jit_solution(13396056482772406992)
XLA Ops:
  0.6 102.1 %attention.1 = (bf16[512,512]{1,0:T(8,128)(2,1)}, bf16[512,512]{1,0:T(8,128)(2,1)}, bf16[512,128]{1,0:T(8,128)(2,1)}, bf16[512,128]{1,0:T(8,128)(2,1)}) custom-call(bf16[64,4096]{1,0:T(8,128)(2,1)} %q_in.1, bf16[64,1024]{1,0:T(8,128)(2,1)} %k_in.1, bf16[64,1024]{1,0:T(8,128)(2,1)} %v_in.1, bf16[64,4096]{1,0:T(8,128)(2,1)} %g_in.1, s32[256,128]{1,0:T(8,128)} %bitcast.1), custom_call_target="tpu_custom_call" | custom-call | flops 3623878656 | bytes 2097152 | tf_op jit(solution)/shard_map/attention/pallas_call | solution.py:537
  102.8 2.2 %hand_over.1 = (bf16[512,512]{1,0:T(8,128)(2,1)}, bf16[512,512]{1,0:T(8,128)(2,1)}, bf16[512,128]{1,0:T(8,128)(2,1)}, bf16[512,128]{1,0:T(8,128)(2,1)}) custom-call(bf16[512,512]{1,0:T(8,128)(2,1)} %get-tuple-element.8.refs_0_, bf16[512,512]{1,0:T(8,128)(2,1)} %get-tuple-element.9.refs_1_, bf16[512,128]{1,0:T(8,128)(2,1)} %get-tuple-element.10.refs_2_, ...), custom_call_target="tpu_custom_call" | custom-call | tf_op jit(solution)/shard_map/hand_over/pallas_call | solution.py:585

commit v4 on v3

--- a/solution.py
+++ b/solution.py
@@ -16,7 +16,7 @@
 CTX = 64
 PLANE = 16
 PLANES = CTX // PLANE
-EARLY = 3
+EARLY = 5
 TP = 8
 HALF = SUB * GROUP
 LANES = 2 * HALF
@@ -168,16 +168,87 @@
             qg_out[j, h] = q_vm[:, at : at + HD]
             qg_out[j, GROUP + h] = g_vm[:, at : at + HD]
 
-    @pl.when(c < 1)
-    def _():
-        kv[:, TOK : 2 * TOK] = jnp.zeros((2, TOK, HD), jnp.bfloat16)
-
-    @pl.when(c < 2)
-    def _():
-        kv[:, 0:TOK] = jnp.zeros((2, TOK, HD), jnp.bfloat16)
-
     kv[:, own_rows(t), :] = kv_out[t]
     qg[t] = qg_out[t]
+
+    pl.semaphore_wait(barrier, arrivals)
+
+    def partner(dz, dc):
+        return ((zh + dz) % 4) * 2 + (co + dc) % 2
+
+    partners = [(1, 0), (3, 0), (1, 1), (3, 1), (2, 0), (2, 1), (0, 1)]
+    across, below, above = (zh + 2) % 4, (zh + 3) % 4, (zh + 1) % 4
+    targets = [zh * 2 + 1 - co, across * 2 + co, across * 2 + 1 - co]
+    targets += [below * 2 + co, above * 2 + co, below * 2 + 1 - co, above * 2 + 1 - co]
+
+    def exchange(src, dst, send, recv, to):
+        return pltpu.make_async_remote_copy(
+            src_ref=src,
+            dst_ref=dst,
+            send_sem=send.at[to],
+            recv_sem=recv.at[t],
+            device_id={"tp": to},
+            device_id_type=MESH,
+        )
+
+    def key_copy(to):
+        return exchange(kv_out.at[to], kv.at[:, own_rows(t)], k_send, k_recv, to)
+
+    def query_copy(to):
+        return exchange(qg_out.at[to], qg.at[t], q_send, q_recv, to)
+
+    def relay_copy(r):
+        return pltpu.make_async_remote_copy(
+            src_ref=kv_out.at[r],
+            dst_ref=relay,
+            send_sem=r_send.at[r],
+            recv_sem=r_recv,
+            device_id={"ctx": first + r + 8 * (15 - p)},
+            device_id_type=MESH,
+        )
+
+    def cross_copy(src):
+        at = jnp.where(p < 8, TOK, 0) + t * SUB
+        return pltpu.make_async_remote_copy(
+            src_ref=src,
+            dst_ref=kv.at[:, pl.ds(pl.multiple_of(at, SUB), SUB)],
+            send_sem=x_send,
+            recv_sem=x_recv.at[jnp.where(p < 8, 0, 8) + t],
+            device_id={"ctx": (plane + 1) % PLANES * PLANE, "tp": p % 8},
+            device_id_type=MESH,
+        )
+
+    @pl.when((p == 15) & crossing)
+    def _():
+        for r in range(TP):
+            relay_copy(r).start()
+
+    @pl.when((p == 14) & crossing)
+    def _():
+        for r in range(TP):
+            if r != 6:
+                relay_copy(r).start()
+        cross_copy(kv_out.at[6]).start()
+
+    for dz, dc in partners:
+        key_copy(partner(dz, dc)).start()
+
+    @pl.when((p != 14) & crossing)
+    def _():
+        pltpu.make_async_copy(relay, relay, r_recv).wait()
+        cross_copy(relay).start()
+
+    for to in targets[:EARLY]:
+        query_copy(to).start()
+
+    @pl.when(c < 1)
+    def _():
+        kv[:, TOK : 2 * TOK] = jnp.zeros((2, TOK, HD), jnp.bfloat16)
+
+    @pl.when(c < 2)
+    def _():
+        kv[:, 0:TOK] = jnp.zeros((2, TOK, HD), jnp.bfloat16)
+
     acc[...] = jnp.zeros_like(acc)
 
     seg_copy.wait()
@@ -199,76 +270,6 @@
         segrow[2 * i] = jnp.concatenate([low, low], 1)
         segrow[2 * i + 1] = jnp.concatenate([high, high], 1)
 
-    pl.semaphore_wait(barrier, arrivals)
-
-    def partner(dz, dc):
-        return ((zh + dz) % 4) * 2 + (co + dc) % 2
-
-    partners = [(1, 0), (3, 0), (1, 1), (3, 1), (2, 0), (2, 1), (0, 1)]
-    to_1, to_2, to_3 = (zh + 1) % 4, (zh + 3) % 4, (zh + 2) % 4
-    targets = [zh * 2 + 1 - co, to_1 * 2 + co, to_2 * 2 + co]
-    targets += [to_1 * 2 + 1 - co, to_2 * 2 + 1 - co, to_3 * 2 + co, to_3 * 2 + 1 - co]
-
-    def exchange(src, dst, send, recv, to):
-        return pltpu.make_async_remote_copy(
-            src_ref=src,
-            dst_ref=dst,
-            send_sem=send.at[to],
-            recv_sem=recv.at[t],
-            device_id={"tp": to},
-            device_id_type=MESH,
-        )
-
-    def key_copy(to):
-        return exchange(kv_out.at[to], kv.at[:, own_rows(t)], k_send, k_recv, to)
-
-    def query_copy(to):
-        return exchange(qg_out.at[to], qg.at[t], q_send, q_recv, to)
-
-    def relay_copy(r):
-        return pltpu.make_async_remote_copy(
-            src_ref=kv_out.at[r],
-            dst_ref=relay,
-            send_sem=r_send.at[r],
-            recv_sem=r_recv,
-            device_id={"ctx": first + r + 8 * (15 - p)},
-            device_id_type=MESH,
-        )
-
-    def cross_copy(src):
-        at = jnp.where(p < 8, TOK, 0) + t * SUB
-        return pltpu.make_async_remote_copy(
-            src_ref=src,
-            dst_ref=kv.at[:, pl.ds(pl.multiple_of(at, SUB), SUB)],
-            send_sem=x_send,
-            recv_sem=x_recv.at[jnp.where(p < 8, 0, 8) + t],
-            device_id={"ctx": (plane + 1) % PLANES * PLANE, "tp": p % 8},
-            device_id_type=MESH,
-        )
-
-    @pl.when((p == 15) & crossing)
-    def _():
-        for r in range(TP):
-            relay_copy(r).start()
-
-    @pl.when((p == 14) & crossing)
-    def _():
-        for r in range(TP):
-            if r != 6:
-                relay_copy(r).start()
-        cross_copy(kv_out.at[6]).start()
-
-    for dz, dc in partners:
-        key_copy(partner(dz, dc)).start()
-
-    @pl.when((p != 14) & crossing)
-    def _():
-        pltpu.make_async_copy(relay, relay, r_recv).wait()
-        cross_copy(relay).start()
-
-    for to in targets[:EARLY]:
-        query_copy(to).start()
-
     def window_copy(d, j):
         return pltpu.make_async_remote_copy(
             src_ref=kv.at[:, own_rows(j)],
@@ -361,10 +362,10 @@
         def _():
             term_copy(part).start()
 
-    early_half = zh < 2
+    outer = (zh == 0) | (zh == 3)
 
     def unit(i, final):
-        dz = i + i // 2 - 2 * (i // 3)
+        dz = jnp.where(i < 2, i * 2, jnp.where((i == 2) == outer, 1, 3))
         sz = (zh + dz) % 4
 
         def arrived(j):
@@ -434,12 +435,6 @@
                 e_scr[tile(n), at] = (p * (slope - delta)).astype(jnp.bfloat16)
             acc[0, keys(n), :] += dot(e_scr[tile(n), :], qs)
             acc[1, keys(n), :] += dot_nt(p_scr[tile(n), :], gst_scr[...])
-            if final and n == 1:
-
-                @pl.when(jnp.logical_not(early_half))
-                def _():
-                    send_terms(0)
-
             if final and n in (3, 5, 7):
                 send_terms(n // 2)
         for half, at in enumerate(halves):
@@ -452,10 +447,7 @@
 
     lax.fori_loop(0, UNITS - 1, one_unit, 0)
 
-    @pl.when(early_half)
-    def _():
-        send_terms(0)
-
+    send_terms(0)
     unit(UNITS - 1, True)
 
     for part, (d, start, size) in enumerate(PARTS):

time: 105 us -> 103 us (0.981)
  the two profiles are of different devices: /device:TPU:15 before, /device:TPU:288 now
where the time goes in v4:
time: 103 us
  Pallas kernels  102 us (99%)
    pallas_call x1, Pallas kernels, on_device(): pl.pallas_call(kernel, out_shape=shapes, in_specs=[hbm, hbm, hbm, hbm, hb...  99.9 us
    pallas_call x1, Pallas kernels, on_device(): pl.pallas_call(hand_over, out_shape=shapes, in_specs=[whole] * 4, out_spe...  2.15 us

profile of v4, /device:TPU:288, one launch (start us, length us, event | category | flops | bytes accessed | tf_op | source)
XLA Modules:
  0.0 102.7 jit_solution(14461554010409535740)
XLA Ops:
  0.6 99.9 %attention.1 = (bf16[512,512]{1,0:T(8,128)(2,1)}, bf16[512,512]{1,0:T(8,128)(2,1)}, bf16[512,128]{1,0:T(8,128)(2,1)}, bf16[512,128]{1,0:T(8,128)(2,1)}) custom-call(bf16[64,4096]{1,0:T(8,128)(2,1)} %q_in.1, bf16[64,1024]{1,0:T(8,128)(2,1)} %k_in.1, bf16[64,1024]{1,0:T(8,128)(2,1)} %v_in.1, bf16[64,4096]{1,0:T(8,128)(2,1)} %g_in.1, s32[256,128]{1,0:T(8,128)} %bitcast.1), custom_call_target="tpu_custom_call" | custom-call | flops 3623878656 | bytes 2097152 | tf_op jit(solution)/shard_map/attention/pallas_call | solution.py:529
  100.6 2.2 %hand_over.1 = (bf16[512,512]{1,0:T(8,128)(2,1)}, bf16[512,512]{1,0:T(8,128)(2,1)}, bf16[512,128]{1,0:T(8,128)(2,1)}, bf16[512,128]{1,0:T(8,128)(2,1)}) custom-call(bf16[512,512]{1,0:T(8,128)(2,1)} %get-tuple-element.8.refs_0_, bf16[512,512]{1,0:T(8,128)(2,1)} %get-tuple-element.9.refs_1_, bf16[512,128]{1,0:T(8,128)(2,1)} %get-tuple-element.10.refs_2_, ...), custom_call_target="tpu_custom_call" | custom-call | tf_op jit(solution)/shard_map/hand_over/pallas_call | solution.py:577

commit v5 on v4

--- a/solution.py
+++ b/solution.py
@@ -371,11 +371,6 @@
         def arrived(j):
             pltpu.make_async_copy(qg.at[j], qg.at[j], q_recv.at[j]).wait()
 
-        if final:
-            arrived(sz * 2 + co)
-        else:
-            pl.when(i > 0)(lambda: arrived(sz * 2 + co))
-        arrived(sz * 2 + 1 - co)
         base = pl.multiple_of(sz * TILE, TILE)
         window = pl.ds(base, WIN)
         halves = [slice(0, HALF), slice(HALF, LANES)]
@@ -386,17 +381,20 @@
         def tile(n):
             return slice(n * TILE, (n + 1) * TILE)
 
-        both = pl.ds(sz * 2, 2)
-        qs = qg[both, :GROUP].reshape(LANES, HD)
-        gs = qg[both, GROUP:].reshape(LANES, HD)
-
         terms = []
         for half, at in enumerate(halves):
-            seg_q = segrow[sz * 2 + half][0:1]
+            j = sz * 2 + half
+            if final:
+                arrived(j)
+            else:
+                pl.when((i > 0) | (co != half))(lambda: arrived(j))
+            qs = qg[j, :GROUP].reshape(HALF, HD)
+            gs = qg[j, GROUP:].reshape(HALF, HD)
+            seg_q = segrow[j][0:1]
             causal = place <= lane + half * SUB
             peak = None
             for n in range(TILES):
-                s = dot_nt(kv[0, keys(n), :], qs[at])
+                s = dot_nt(kv[0, keys(n), :], qs)
                 seg_k = segcol[keys(n), :]
                 allowed = jnp.concatenate([seg_k, seg_k], 1) == seg_q
                 if n == TILES - 1:
@@ -416,10 +414,12 @@
             inverse = 1.0 / jnp.sum(total, axis=0, keepdims=True)
 
             attended = dot(kvt[1, :, window], p_scr[:, at]) * inverse
-            gst = (gs[at].astype(jnp.float32).T * inverse).astype(jnp.bfloat16)
+            gst = (gs.astype(jnp.float32).T * inverse).astype(jnp.bfloat16)
             delta = jnp.sum(gst.astype(jnp.float32) * attended, axis=0, keepdims=True)
             gst_scr[:, at] = gst
             terms.append((attended, gst, delta))
+
+        qs = qg[pl.ds(sz * 2, 2), :GROUP].reshape(LANES, HD)
 
         def store(ref, half, value):
             value = value.T.astype(jnp.bfloat16)

time: 103 us -> 104 us (level)
  no operation moved by 1% of the time
where the time goes in v5:
time: 104 us
  Pallas kernels  103 us (99%)
    pallas_call x1, Pallas kernels, on_device(): pl.pallas_call(kernel, out_shape=shapes, in_specs=[hbm, hbm, hbm, hbm, hb...  101 us
    pallas_call x1, Pallas kernels, on_device(): pl.pallas_call(hand_over, out_shape=shapes, in_specs=[whole] * 4, out_spe...  2.15 us

profile of v5, /device:TPU:288, one launch (start us, length us, event | category | flops | bytes accessed | tf_op | source)
XLA Modules:
  0.0 103.8 jit_solution(13310724056789092215)
XLA Ops:
  0.6 101.0 %attention.1 = (bf16[512,512]{1,0:T(8,128)(2,1)}, bf16[512,512]{1,0:T(8,128)(2,1)}, bf16[512,128]{1,0:T(8,128)(2,1)}, bf16[512,128]{1,0:T(8,128)(2,1)}) custom-call(bf16[64,4096]{1,0:T(8,128)(2,1)} %q_in.1, bf16[64,1024]{1,0:T(8,128)(2,1)} %k_in.1, bf16[64,1024]{1,0:T(8,128)(2,1)} %v_in.1, bf16[64,4096]{1,0:T(8,128)(2,1)} %g_in.1, s32[256,128]{1,0:T(8,128)} %bitcast.1), custom_call_target="tpu_custom_call" | custom-call | flops 3623878656 | bytes 2097152 | tf_op jit(solution)/shard_map/attention/pallas_call | solution.py:529
  101.6 2.2 %hand_over.1 = (bf16[512,512]{1,0:T(8,128)(2,1)}, bf16[512,512]{1,0:T(8,128)(2,1)}, bf16[512,128]{1,0:T(8,128)(2,1)}, bf16[512,128]{1,0:T(8,128)(2,1)}) custom-call(bf16[512,512]{1,0:T(8,128)(2,1)} %get-tuple-element.8.refs_0_, bf16[512,512]{1,0:T(8,128)(2,1)} %get-tuple-element.9.refs_1_, bf16[512,128]{1,0:T(8,128)(2,1)} %get-tuple-element.10.refs_2_, ...), custom_call_target="tpu_custom_call" | custom-call | tf_op jit(solution)/shard_map/hand_over/pallas_call | solution.py:577
